TPU v7x, 32 devices: a whole 2x2x4 slice. The times are simulated.
32 devices in a mesh: rep: 4 (over z), fsdp: 8 (over y, x, core).
Axes of the slice: x: 2, y: 2, z: 4, core: 2. Of those that a mesh axis runs over, the one named last changes fastest.
Arguments:
- layer_input: bfloat16 [16, 1024, 768], P('rep', 'fsdp'), may hold values from -40 to 40
- positions: int32 [16, 1024], P('rep', 'fsdp'), may hold values from 0 to 1023, as said below
- cotangent: bfloat16 [16, 1024, 768], P('rep', 'fsdp'), may hold values from -6 to 6
- w_qkv: bfloat16 [768, 2304], P('fsdp'), may hold values from -4 to 4
- w_out: bfloat16 [768, 768], P('fsdp'), may hold values from -1.75 to 1.75
- w_up: bfloat16 [768, 3072], P('fsdp'), may hold values from -0.21875 to 0.21875
- w_down: bfloat16 [768, 3072], P('fsdp'), may hold values from -0.109375 to 0.109375
- ln1_gain: bfloat16 [768], P('fsdp'), may hold values from 0.5 to 1.5
- ln1_bias: bfloat16 [768], P('fsdp'), may hold values from -1.5 to 1.5
- ln2_gain: bfloat16 [768], P('fsdp'), may hold values from 0.5 to 1.5
- ln2_bias: bfloat16 [768], P('fsdp'), may hold values from -1.5 to 1.5
- qkv_bias: bfloat16 [2304], P('fsdp'), may hold values from -2.5 to 2.5
- out_bias: bfloat16 [768], P('fsdp'), may hold values from -2.5 to 2.5
- up_bias: bfloat16 [3072], P('fsdp'), may hold values from -2.5 to 2.5
- down_bias: bfloat16 [768], P('fsdp'), may hold values from -2.5 to 2.5
Outputs:
- output: bfloat16 [16, 1024, 768], P('rep', 'fsdp')
- grad_input: bfloat16 [16, 1024, 768], P('rep', 'fsdp')
- grad_w_qkv: float32 [768, 2304], P('fsdp')
- grad_w_out: float32 [768, 768], P('fsdp')
- grad_w_up: float32 [768, 3072], P('fsdp')
- grad_w_down: float32 [768, 3072], P('fsdp')
- grad_ln1_gain: float32 [768], P('fsdp')
- grad_ln1_bias: float32 [768], P('fsdp')
- grad_ln2_gain: float32 [768], P('fsdp')
- grad_ln2_bias: float32 [768], P('fsdp')
- grad_qkv_bias: float32 [2304], P('fsdp')
- grad_out_bias: float32 [768], P('fsdp')
- grad_up_bias: float32 [3072], P('fsdp')
- grad_down_bias: float32 [768], P('fsdp')
Inputs may be any that keep to these rules, and one draw needn't show every extreme that they name: positions[s, 0] is 0, and each later positions[s, t] is either 0 or positions[s, t - 1] + 1; sequence 0 is one document of 1024 tokens.
All inputs are finite; a program needn't handle non-finite values.
Results may differ from a plain program's by a relative error of at most 0.0093.
Values may be sent and summed in bfloat16 or wider, within the bound.
No kernel may reach another device: no remote copies, remote signals or barrier semaphores. Data moves between devices by JAX's collectives and lax.ppermute only.
A program may use at most 320 MiB of HBM per device.

v0:
```python
import jax
import jax.numpy as jnp
from jax import lax
from jax.sharding import PartitionSpec as P

H = 12
HD = 64
ROT = 16
EPS = 1e-05
NEG = -1e30


def norm_rows(values, gain, shift):
    mean = jnp.mean(values, axis=-1, keepdims=True)
    centred = values - mean
    spread = jnp.mean(centred * centred, axis=-1, keepdims=True)
    return centred * lax.rsqrt(spread + EPS) * gain + shift


def rotate(values, cosine, sine):
    half = ROT // 2
    head = values[..., :ROT]
    turned = jnp.concatenate([-head[..., half:], head[..., :half]], axis=-1)
    return jnp.concatenate([head * cosine + turned * sine, values[..., ROT:]], axis=-1)


def angles(positions):
    inverse = 10000.0 ** (-jnp.arange(0, ROT, 2, dtype=jnp.float32) / ROT)
    phase = positions.astype(jnp.float32)[..., None] * inverse
    phase = jnp.concatenate([phase, phase], axis=-1)[..., None, :]
    return (jnp.cos(phase), jnp.sin(phase))


def on_device(
    layer_input,
    positions,
    cotangent,
    w_qkv,
    w_out,
    w_up,
    w_down,
    ln1_gain,
    ln1_bias,
    ln2_gain,
    ln2_bias,
    qkv_bias,
    out_bias,
    up_bias,
    down_bias,
):
    seq_count, span_len, width = layer_input.shape
    shard_count = lax.axis_size("fsdp")
    shard_index = lax.axis_index("fsdp")
    row_count = seq_count * span_len
    qkv_cols = w_qkv.shape[1]
    hidden_cols = w_up.shape[1]
    vectors = (
        lax.all_gather(ln1_gain, "fsdp", axis=0, tiled=True),
        lax.all_gather(ln1_bias, "fsdp", axis=0, tiled=True),
        lax.all_gather(ln2_gain, "fsdp", axis=0, tiled=True),
        lax.all_gather(ln2_bias, "fsdp", axis=0, tiled=True),
        lax.all_gather(qkv_bias, "fsdp", axis=0, tiled=True),
        lax.all_gather(out_bias, "fsdp", axis=0, tiled=True),
        lax.all_gather(up_bias, "fsdp", axis=0, tiled=True),
        lax.all_gather(down_bias, "fsdp", axis=0, tiled=True),
    )
    gain_one, shift_one, gain_two, shift_two, bias_qkv, bias_out, bias_up, bias_down = [
        v.astype(jnp.float32) for v in vectors
    ]
    source = layer_input.reshape(row_count, width).astype(jnp.float32)
    normed_one, pull_one = jax.vjp(norm_rows, source, gain_one, shift_one)
    normed_two, pull_two = jax.vjp(norm_rows, source, gain_two, shift_two)
    input_one = normed_one.astype(jnp.bfloat16)
    input_two = normed_two.astype(jnp.bfloat16)
    pieces = (
        lax.all_gather(w_qkv, "fsdp", axis=0, tiled=True),
        lax.all_gather(w_up, "fsdp", axis=0, tiled=True),
    )
    count = pieces[0].shape[0]
    qkv_sum = jnp.dot(input_one, pieces[0], preferred_element_type=jnp.float32)
    up_sum = jnp.dot(input_two, pieces[1], preferred_element_type=jnp.float32)
    qkv_full = qkv_sum + bias_qkv
    up_full = up_sum + bias_up
    cosine, sine = angles(positions)

    def turn_all(packed):
        shaped = packed.reshape(seq_count, span_len, 3, H, HD)
        return (
            rotate(shaped[:, :, 0], cosine, sine),
            rotate(shaped[:, :, 1], cosine, sine),
            shaped[:, :, 2],
        )

    turned, pull_turn = jax.vjp(turn_all, qkv_full)
    query_low = turned[0].astype(jnp.bfloat16)
    key_low = turned[1].astype(jnp.bfloat16)
    value_low = turned[2].astype(jnp.bfloat16)
    key_flat = key_low.reshape(seq_count, span_len, width)
    value_flat = value_low.reshape(seq_count, span_len, width)
    query_index = shard_index * span_len + jnp.arange(span_len, dtype=jnp.int32)
    first_seen = query_index[None, :] - positions

    def scores_with(key_piece):
        count = key_piece.shape[1]
        keys = key_piece.reshape(seq_count, count, H, HD)
        raw = (
            jnp.einsum("sqhd,skhd->shqk", query_low, keys, preferred_element_type=jnp.float32)
            * 0.125
        )
        key_index = jnp.arange(count, dtype=jnp.int32)
        seen = (key_index[None, None, :] <= query_index[None, :, None]) & (
            key_index[None, None, :] >= first_seen[:, :, None]
        )
        return (raw, seen[:, None])

    start_top = jnp.full((seq_count, H, span_len), NEG, jnp.float32)
    raw, seen = scores_with(lax.all_gather(key_flat, "fsdp", axis=1, tiled=True))
    masked = jnp.where(seen, raw, NEG)
    new_top = jnp.maximum(start_top, jnp.max(masked, axis=-1))
    weights = jnp.where(seen, jnp.exp(masked - new_top[..., None]), 0.0)
    total = jnp.sum(weights, axis=-1)
    log_total = new_top + jnp.log(total)
    pieces = (
        lax.all_gather(key_flat, "fsdp", axis=1, tiled=True),
        lax.all_gather(value_flat, "fsdp", axis=1, tiled=True),
    )
    raw, seen = scores_with(pieces[0])
    count = pieces[1].shape[1]
    values = pieces[1].reshape(seq_count, count, H, HD)
    probs = jnp.where(seen, jnp.exp(raw - log_total[..., None]), 0.0)
    probs_low = probs.astype(jnp.bfloat16)
    residue = (probs - probs_low.astype(jnp.float32)).astype(jnp.bfloat16)
    mixed_sum = jnp.einsum("shqk,skhd->sqhd", probs_low, values, preferred_element_type=jnp.float32)
    residue_sum = jnp.einsum("shqk,skhd->sqhd", residue, values, preferred_element_type=jnp.float32)
    attended = mixed_sum.reshape(row_count, width).astype(jnp.bfloat16)
    hidden = jax.nn.gelu(up_full, approximate=False).astype(jnp.bfloat16)
    pieces = (
        lax.all_gather(w_out, "fsdp", axis=0, tiled=True),
        lax.all_gather(w_down, "fsdp", axis=0, tiled=True),
    )
    columns = jnp.einsum("rk,ck->rc", attended, pieces[0], preferred_element_type=jnp.float32)
    columns = columns + jnp.einsum(
        "rk,ck->rc", hidden, pieces[1], preferred_element_type=jnp.float32
    )
    output = (
        (source + columns + bias_out + bias_down).astype(jnp.bfloat16).reshape(layer_input.shape)
    )
    grad_out = cotangent.reshape(row_count, width)
    pieces = (
        lax.all_gather(w_out, "fsdp", axis=0, tiled=True),
        lax.all_gather(w_down, "fsdp", axis=0, tiled=True),
    )
    count = pieces[0].shape[0]
    grad_attended = jnp.dot(grad_out, pieces[0], preferred_element_type=jnp.float32)
    grad_hidden = jnp.dot(grad_out, pieces[1], preferred_element_type=jnp.float32)
    grad_mixed = grad_attended.astype(jnp.bfloat16)
    gelu_value, pull_gelu = jax.vjp(lambda v: jax.nn.gelu(v, approximate=False), up_full)
    grad_up = pull_gelu(grad_hidden)[0].astype(jnp.bfloat16)
    grad_heads = grad_mixed.reshape(seq_count, span_len, H, HD)
    carried = jnp.sum(grad_heads.astype(jnp.float32) * (mixed_sum + residue_sum), axis=-1)
    carried_rows = jnp.transpose(carried, (0, 2, 1))
    pieces = (
        lax.all_gather(key_flat, "fsdp", axis=1, tiled=True),
        lax.all_gather(value_flat, "fsdp", axis=1, tiled=True),
    )
    raw, seen = scores_with(pieces[0])
    count = pieces[0].shape[1]
    keys = pieces[0].reshape(seq_count, count, H, HD)
    values = pieces[1].reshape(seq_count, count, H, HD)
    probs = jnp.where(seen, jnp.exp(raw - log_total[..., None]), 0.0)
    probs_low = probs.astype(jnp.bfloat16)
    grad_probs = jnp.einsum(
        "sqhd,skhd->shqk", grad_heads, values, preferred_element_type=jnp.float32
    )
    grad_scores = (probs * (grad_probs - carried_rows[..., None])).astype(jnp.bfloat16)
    grad_query = jnp.einsum(
        "shqk,skhd->sqhd", grad_scores, keys, preferred_element_type=jnp.float32
    )
    key_part = jnp.einsum(
        "shqk,sqhd->skhd", grad_scores, query_low, preferred_element_type=jnp.float32
    )
    value_part = jnp.einsum(
        "shqk,sqhd->skhd", probs_low, grad_heads, preferred_element_type=jnp.float32
    )
    both = jnp.concatenate(
        [key_part.reshape(seq_count, count, width), value_part.reshape(seq_count, count, width)],
        axis=2,
    )
    key_terms = both
    grad_query, key_terms = (grad_query, key_terms)
    grad_query = grad_query * 0.125
    key_owned = lax.psum_scatter(key_terms, "fsdp", scatter_dimension=1, tiled=True)
    grad_key = key_owned[..., :width].reshape(seq_count, span_len, H, HD) * 0.125
    grad_value = key_owned[..., width:].reshape(seq_count, span_len, H, HD)
    grad_qkv = pull_turn((grad_query, grad_key, grad_value))[0].astype(jnp.bfloat16)
    pieces = (
        lax.all_gather(w_qkv, "fsdp", axis=0, tiled=True),
        lax.all_gather(w_up, "fsdp", axis=0, tiled=True),
    )
    columns_one = jnp.einsum("rk,ck->rc", grad_qkv, pieces[0], preferred_element_type=jnp.float32)
    columns_two = jnp.einsum("rk,ck->rc", grad_up, pieces[1], preferred_element_type=jnp.float32)
    grad_source_one, grad_gain_one, grad_shift_one = pull_one(columns_one)
    grad_source_two, grad_gain_two, grad_shift_two = pull_two(columns_two)
    grad_out_float = grad_out.astype(jnp.float32)
    grad_input = (
        (grad_out_float + grad_source_one + grad_source_two)
        .astype(jnp.bfloat16)
        .reshape(layer_input.shape)
    )
    grad_out_total = jnp.sum(grad_out_float, axis=0)
    local_vectors = (
        grad_gain_one,
        grad_shift_one,
        grad_gain_two,
        grad_shift_two,
        jnp.sum(grad_qkv.astype(jnp.float32), axis=0),
        grad_out_total,
        jnp.sum(grad_up.astype(jnp.float32), axis=0),
    )
    summed = lax.psum(
        (
            local_vectors[0],
            local_vectors[1],
            local_vectors[2],
            local_vectors[3],
            local_vectors[4],
            local_vectors[5],
            local_vectors[6],
        ),
        ("rep", "fsdp"),
    )
    owned_vectors = [
        lax.dynamic_slice_in_dim(
            v, shard_index * (v.shape[0] // shard_count), v.shape[0] // shard_count
        )
        for v in summed
    ]
    owned = lax.psum_scatter(
        jnp.concatenate(
            [
                jnp.einsum("rc,rk->ck", input_one, grad_qkv, preferred_element_type=jnp.float32),
                jnp.einsum("rc,rk->ck", grad_out, attended, preferred_element_type=jnp.float32),
                jnp.einsum("rc,rk->ck", input_two, grad_up, preferred_element_type=jnp.float32),
                jnp.einsum("rc,rk->ck", grad_out, hidden, preferred_element_type=jnp.float32),
            ],
            axis=1,
        ),
        "fsdp",
        scatter_dimension=0,
        tiled=True,
    )
    owned = lax.psum(owned, "rep")
    edge_two = qkv_cols + width
    edge_three = edge_two + hidden_cols
    grad_w_qkv = owned[:, :qkv_cols]
    grad_w_out = owned[:, qkv_cols:edge_two]
    grad_w_up = owned[:, edge_two:edge_three]
    grad_w_down = owned[:, edge_three:]
    return (
        output,
        grad_input,
        grad_w_qkv,
        grad_w_out,
        grad_w_up,
        grad_w_down,
        owned_vectors[0],
        owned_vectors[1],
        owned_vectors[2],
        owned_vectors[3],
        owned_vectors[4],
        owned_vectors[5],
        owned_vectors[6],
        owned_vectors[5],
    )


def solution(mesh):
    return jax.shard_map(
        on_device,
        mesh=mesh,
        in_specs=(
            P("rep", "fsdp", None),
            P("rep", "fsdp"),
            P("rep", "fsdp", None),
            P("fsdp", None),
            P("fsdp", None),
            P("fsdp", None),
            P("fsdp", None),
            P("fsdp"),
            P("fsdp"),
            P("fsdp"),
            P("fsdp"),
            P("fsdp"),
            P("fsdp"),
            P("fsdp"),
            P("fsdp"),
        ),
        out_specs=(
            P("rep", "fsdp", None),
            P("rep", "fsdp", None),
            P("fsdp", None),
            P("fsdp", None),
            P("fsdp", None),
            P("fsdp", None),
            P("fsdp"),
            P("fsdp"),
            P("fsdp"),
            P("fsdp"),
            P("fsdp"),
            P("fsdp"),
            P("fsdp"),
            P("fsdp"),
        ),
        check_vma=False,
    )
```

profile of v0, /device:TPU:0, one launch (start us, length us, event | category | flops | bytes accessed | tf_op | source)
XLA Modules:
  0.0 780.7 jit_solution(14124956346842506521)
XLA Ops:
  21.0 26.5 %all-reduce.19 = (bf16[768]{0:T(1024)(128)(2,1)S(1)}, bf16[768]{0:T(1024)(128)(2,1)S(1)}, bf16[768]{0:T(1024)(128)(2,1)}, bf16[768]{0:T(1024)(128)(2,1)}, bf16[7...) all-reduce(bf16[768]{0:T(1024)(128)(2,1)S(1)} %dynamic-update-slice, ...), channel_id=1, replica_groups=mesh['rep'=4,'fsdp'=8] {'fsdp'}, use_global_device_ids=true, to_apply=%add.15 | all-reduce | flops 6912 | bytes 27648
  49.2 6.1 convolution_add_fusion
  55.4 6.2 copy.46
  61.5 6.3 reshape.249
  84.6 37.4 %all-gather.12.cloned.1.call-done = bf16[4,1024,768]{1,2,0:T(8,128)(2,1)} async-done(((bf16[4,128,768]{1,2,0:T(8,128)(2,1)}), bf16[4,1024,768]{1,2,0:T(8,128)(2,1)}) %all-gather.12.cloned.1.call-update) | async-done | bytes 6291472 | tf_op jit(solution)/shard_map/all_gather | solution.py:124
  121.9 12.9 %select_reduce_fusion.1 = (f32[4,12,128]{2,1,0:T(8,128)S(1)}, f32[4,12,128,1024]{3,2,1,0:T(8,128)}) fusion(pred[4,128,1024]{2,1,0:T(8,128)(4,1)S(1)} %fusion.13, bf16[4,1024,12,64]{1,3,2,0:T(8,128)(2,1)} %bitcast.164, bf16[4,128,12,48]{1,3,2,0:T(8,128)(2,1)S(1)} %slice.110, bf16[4,128,12,16]{1,3,2,0:T(8,128)(2,1)S(1)} %get-tuple-element.61), kind=kOutput, calls=%fused_computation.6 | convolution fusion | flops 825747456 | bytes 32792576 | tf_op jit(solution)/shard_map/sqhd,skhd->shqk/dot_general | solution.py:107
  134.9 12.2 %select_reduce_fusion = f32[4,12,128]{2,1,0:T(8,128)S(1)} fusion(f32[4,12,128,1024]{3,2,1,0:T(8,128)} %get-tuple-element.76, f32[4,12,128]{2,1,0:T(8,128)S(1)} %broadcast_maximum_fusion, pred[4,128,1024]{2,1,0:T(8,128)(4,1)S(1)} %fusion.13), kind=kLoop, calls=%fused_computation.5 | loop fusion | flops 31451136 | bytes 25739264 | tf_op jit(solution)/shard_map/reduce_sum | solution.py:121
  147.1 23.9 %all-gather.10.cloned.1.call-done = bf16[4,1024,768]{1,2,0:T(8,128)(2,1)} async-done(((bf16[4,128,768]{1,2,0:T(8,128)(2,1)}), bf16[4,1024,768]{1,2,0:T(8,128)(2,1)}) %all-gather.10.cloned.1.call-update) | async-done | bytes 6291472 | tf_op jit(solution)/shard_map/all_gather | solution.py:125
  170.9 14.2 %fusion.58 = f32[4,12,64,128]{3,2,1,0:T(8,128)} fusion(bf16[4,1024,12,64]{1,3,2,0:T(8,128)(2,1)} %bitcast.190, f32[4,12,128,1024]{3,2,1,0:T(8,128)} %get-tuple-element.76, f32[4,12,128]{2,1,0:T(8,128)S(1)} %log_add_fusion, pred[4,128,1024]{2,1,0:T(8,128)(4,1)S(1)} %fusion.13), kind=kOutput, calls=%fused_computation.110 | convolution fusion | flops 830472192 | bytes 33579008 | tf_op jit(solution)/shard_map/shqk,skhd->sqhd/dot_general | solution.py:133
  185.2 15.0 %fusion.16 = f32[4,128,12]{1,2,0:T(8,128)S(1)} fusion(f32[4,12,64,128]{3,2,1,0:T(8,128)} %fusion.58, bf16[4,1024,12,64]{1,3,2,0:T(8,128)(2,1)} %bitcast.191, f32[4,12,128,1024]{3,2,1,0:T(8,128)} %get-tuple-element.76, f32[4,12,128]{2,1,0:T(8,128)S(1)} %log_add_fusion, pred[4,128,1024]{2,1,0:T(8,128)(4,1)S(1)} %fusion.13, bf16[4,128,12,64]{1,0,3,2:T(4,128)(2,1)} %reshape.254), kind=kOutput, calls=%fused_computation.48 | convolution fusion | flops 850913280 | bytes 34390016 | tf_op jit(solution)/shard_map/shqk,skhd->sqhd/dot_general | solution.py:134
  200.2 20.5 %multiply_convert_fusion = bf16[4,12,128,1024]{3,2,1,0:T(8,128)(2,1)} fusion(f32[4,12,128,1024]{3,2,1,0:T(8,128)} %get-tuple-element.76, f32[4,12,128]{2,1,0:T(8,128)S(1)} %bitcast.194, f32[4,12,128]{2,1,0:T(8,128)S(1)} %log_add_fusion, pred[4,128,1024]{2,1,0:T(8,128)(4,1)S(1)} %fusion.13, bf16[4,1024,12,64]{1,3,2,0:T(8,128)(2,1)} %bitcast.192, ...), kind=kOutput, calls=%fused_computation.2 | convolution fusion | flops 843055104 | bytes 45400064 | tf_op jit(solution)/shard_map/sqhd,skhd->shqk/dot_general | solution.py:172
  220.6 11.1 %fusion.50 = f32[4,12,64,1024]{3,2,1,0:T(8,128)} fusion(bf16[4,12,128,1024]{3,2,1,0:T(8,128)(2,1)} %multiply_convert_fusion, bf16[4,128,12,48]{1,3,2,0:T(8,128)(2,1)S(1)} %slice.110, bf16[4,128,12,16]{1,3,2,0:T(8,128)(2,1)S(1)} %get-tuple-element.61), kind=kOutput, calls=%fused_computation.98 | convolution fusion | flops 806879232 | bytes 25952256 | tf_op jit(solution)/shard_map/shqk,sqhd->skhd/dot_general | solution.py:179
  231.8 14.8 %fusion.47 = f32[4,12,64,1024]{3,2,1,0:T(8,128)} fusion(bf16[4,128,12,64]{1,0,3,2:T(4,128)(2,1)S(1)} %copy-done.12, f32[4,12,128,1024]{3,2,1,0:T(8,128)} %get-tuple-element.76, f32[4,12,128]{2,1,0:T(8,128)S(1)} %log_add_fusion, pred[4,128,1024]{2,1,0:T(8,128)(4,1)S(1)} %fusion.13), kind=kOutput, calls=%fused_computation.94 | convolution fusion | flops 830472192 | bytes 39084032 | tf_op jit(solution)/shard_map/shqk,sqhd->skhd/dot_general | solution.py:182
  246.5 18.8 %pad_maximum_fusion.1 = f32[4,1024,1536]{1,2,0:T(8,128)} fusion(f32[4,1024,768]{1,2,0:T(8,128)} %bitcast.163, f32[4,1024,768]{1,2,0:T(8,128)} %bitcast.162), kind=kLoop, calls=%fused_computation.1 | loop fusion | flops 6291456 | bytes 50331648 | tf_op jit(solution)/shard_map/concatenate | solution.py:185
  266.0 9.4 %all-gather = bf16[8,1,384]{2,1,0:T(2,128)(2,1)S(1)} all-gather(bf16[1,1,384]{2,1,0:T(2,128)(2,1)S(1)} %reshape.280), channel_id=1, replica_groups=mesh['rep'=4,'fsdp'=8] {'fsdp'}, dimensions={0}, use_global_device_ids=true | all-gather | bytes 6912 | tf_op jit(solution)/shard_map/all_gather | solution.py:64
  276.7 8.9 %fusion.83 = f32[512,3072]{1,0:T(8,128)} fusion(bf16[512,768]{1,0:T(8,128)(2,1)S(1)} %get-tuple-element.54, bf16[768,3072]{1,0:T(8,128)(2,1)} %all-gather.16.cloned.1.call-done), kind=kOutput, calls=%fused_computation.154 | convolution fusion | flops 2415919104 | bytes 11796480 | tf_op jit(solution)/shard_map/dot_general | solution.py:81
  285.6 19.4 %convert_reduce_fusion = (f32[3072]{0:T(1024)S(1)}, bf16[512,3072]{1,0:T(8,128)(2,1)S(1)}, f32[512,3072]{1,0:T(8,128)S(1)}) fusion(f32[512,3072]{1,0:T(8,128)} %fusion.83, f32[3072]{0:T(1024)S(1)} %bitcast.188, bf16[512,768]{1,0:T(8,128)(2,1)S(1)} %bitcast.170, bf16[768,3072]{1,0:T(8,128)(2,1)} %all-gather.18.cloned.1.call-done), kind=kOutput, calls=%fused_computation.12 | convolution fusion | flops 2533880832 | bytes 21258240 | tf_op jit(solution)/shard_map/dot_general | solution.py:155
  305.0 3.2 multiply_convert_fusion.1
  308.2 7.8 convolution_bitcast_fusion
  316.0 5.2 fusion.86
  321.2 11.3 %multiply_bitcast_fusion = f32[4,128,12,64]{1,3,2,0:T(8,128)S(1)} fusion(bf16[4,1024,12,64]{1,3,2,0:T(8,128)(2,1)} %bitcast.165, bf16[4,12,128,1024]{3,2,1,0:T(8,128)(2,1)} %multiply_convert_fusion), kind=kOutput, calls=%fused_computation.82 | convolution fusion | flops 805699584 | bytes 20447232 | tf_op jit(solution)/shard_map/shqk,skhd->sqhd/dot_general | solution.py:176
  340.6 82.4 %reduce-scatter.3.cloned.1.call-done = f32[4,128,1536]{1,2,0:T(8,128)} async-done(((f32[4,1024,1536]{1,2,0:T(8,128)}), f32[4,128,1536]{1,2,0:T(8,128)}) %reduce-scatter.3.cloned.1.call-update) | async-done | bytes 3145744 | tf_op jit(solution)/shard_map/reduce_scatter | solution.py:192
  431.2 4.9 fusion.9
  436.1 19.4 %pad_maximum_fusion = f32[768,9216]{1,0:T(8,128)} fusion(f32[768,3072]{1,0:T(8,128)} %convolution_bitcast_fusion, f32[768,3072]{1,0:T(8,128)} %fusion.86, f32[768,768]{1,0:T(8,128)S(1)} %copy.57, f32[768,2304]{1,0:T(8,128)} %fusion.9), kind=kLoop, calls=%fused_computation | loop fusion | flops 21233664 | bytes 56623104 | tf_op jit(solution)/shard_map/concatenate | solution.py:239
  456.4 172.6 %reduce-scatter.5.cloned.1.call-done = f32[96,9216]{1,0:T(8,128)} async-done(((f32[768,9216]{1,0:T(8,128)}), f32[96,9216]{1,0:T(8,128)}) %reduce-scatter.5.cloned.1.call-update) | async-done | bytes 3538960 | tf_op jit(solution)/shard_map/reduce_scatter | solution.py:238
  629.0 6.1 fusion.85
  635.1 5.8 fusion.84
  642.9 5.4 fusion.76
  650.8 44.4 %all-reduce.18 = (f32[768]{0:T(1024)S(1)}, f32[768]{0:T(1024)S(1)}, f32[768]{0:T(1024)S(1)}, f32[768]{0:T(1024)S(1)}, f32[2304]{0:T(1024)S(1)}, /*index=5*/f32[768]{0:T(1024)S(1)}, f32[3072]{0:T(1024)S(1)}) all-reduce(f32[768]{0:T(1024)S(1)} %get-tuple-element.23, ...), channel_id=1, replica_groups=mesh['rep'=4,'fsdp'=8] {'rep','fsdp'}, use_global_device_ids=true, to_apply=%region_13.14 | all-reduce | flops 9216 | bytes 73728 | tf_op jit(solution)/shard_map/psum | solution.py:220
  698.9 3.0 add_convert_fusion.2
  701.9 64.2 %all-reduce.22.cloned.1.call-done = f32[96,9216]{1,0:T(8,128)} async-done(((f32[96,9216]{1,0:T(8,128)}), f32[96,9216]{1,0:T(8,128)}) %all-reduce.22.cloned.1.call-update) | async-done | bytes 3538960 | tf_op jit(solution)/shard_map/psum | solution.py:252
  766.1 3.3 fusion.79
  (176 shorter events, 62.0 us)
Async XLA Ops:
  7.2 42.0 %all-gather.8.cloned.1.call-start = ((), (), s32[]{:S(2)}) async-start(), calls=%async_computation.2 | async-start | bytes 3981312 | tf_op jit(solution)/shard_map/all_gather | solution.py:76
  7.9 69.8 %all-gather.14.cloned.1.call-start = ((), (), s32[]{:S(2)}) async-start(), calls=%async_computation.5 | async-start | bytes 1327104 | tf_op jit(solution)/shard_map/all_gather | solution.py:138
  8.7 113.3 %all-gather.12.cloned.1.call-start = ((), (), s32[]{:S(2)}) async-start(), calls=%async_computation.4 | async-start | bytes 7077888 | tf_op jit(solution)/shard_map/all_gather | solution.py:124
  10.0 45.3 %copy-start.23 = (f32[512]{0:T(512)}, f32[512]{0:T(512)S(1)}, u32[]{:S(2)}) copy-start(f32[512]{0:T(512)S(1)} %get-tuple-element.73) | copy-start | bytes 6148
  11.6 263.9 %copy-start.27 = (f32[4,128]{1,0:T(4,128)}, f32[4,128]{1,0:T(4,128)S(1)}, u32[]{:S(2)}) copy-start(f32[4,128]{1,0:T(4,128)S(1)} %fusion.28) | copy-start | bytes 6148
  12.5 58.2 %copy-start.15 = (f32[4,128,16]{1,2,0:T(8,128)}, f32[4,128,16]{1,2,0:T(8,128)S(1)}, u32[]{:S(2)}) copy-start(f32[4,128,16]{1,2,0:T(8,128)S(1)} %get-tuple-element.67) | copy-start | bytes 98308
  12.5 58.2 %copy-start.17 = (f32[4,128,16]{1,2,0:T(8,128)}, f32[4,128,16]{1,2,0:T(8,128)S(1)}, u32[]{:S(2)}) copy-start(f32[4,128,16]{1,2,0:T(8,128)S(1)} %get-tuple-element.68) | copy-start | bytes 98308
  47.5 228.0 %copy-start.19 = (f32[768]{0:T(1024)}, f32[768]{0:T(1024)S(1)}, u32[]{:S(2)}) copy-start(f32[768]{0:T(1024)S(1)} %convert_element_type.126) | copy-start | bytes 9220
  47.5 7.9 %copy-start.21 = (f32[768]{0:T(1024)}, f32[768]{0:T(1024)S(1)}, u32[]{:S(2)}) copy-start(f32[768]{0:T(1024)S(1)} %convert_element_type.137) | copy-start | bytes 9220
  47.6 7.8 copy-start.25
  71.7 6.0 copy-start.5
  72.8 98.1 %all-gather.10.cloned.1.call-start = ((), (), s32[]{:S(2)}) async-start(), calls=%async_computation.3 | async-start | bytes 7077888 | tf_op jit(solution)/shard_map/all_gather | solution.py:125
  75.6 201.1 %all-gather.16.cloned.1.call-start = ((), (), s32[]{:S(2)}) async-start(), calls=%async_computation.6 | async-start | bytes 5308416 | tf_op jit(solution)/shard_map/all_gather | solution.py:77
  76.2 209.3 %all-gather.18.cloned.1.call-start = ((), (), s32[]{:S(2)}) async-start(), calls=%async_computation.7 | async-start | bytes 5308416 | tf_op jit(solution)/shard_map/all_gather | solution.py:139
  76.8 346.2 %reduce-scatter.3.cloned.1.call-start = ((), (), s32[]{:S(2)}) async-start(), calls=%async_computation.8 | async-start | bytes 28311552 | tf_op jit(solution)/shard_map/reduce_scatter | solution.py:192
  220.6 11.1 %copy-start.12 = (bf16[4,128,12,64]{1,0,3,2:T(4,128)(2,1)S(1)}, bf16[4,128,12,64]{1,0,3,2:T(4,128)(2,1)}, u32[]{:S(2)}) copy-start(bf16[4,128,12,64]{1,0,3,2:T(4,128)(2,1)} %reshape.254) | copy-start | bytes 2359300
  265.3 10.1 %copy-start = (bf16[4,128,768]{2,1,0:T(8,128)(2,1)S(1)}, bf16[4,128,768]{2,1,0:T(8,128)(2,1)}, u32[]{:S(2)}) copy-start(bf16[4,128,768]{2,1,0:T(8,128)(2,1)} %param.15) | copy-start | bytes 2359300
  265.3 363.6 %reduce-scatter.5.cloned.1.call-start = ((), (), s32[]{:S(2)}) async-start(), calls=%async_computation.9 | async-start | bytes 31850496 | tf_op jit(solution)/shard_map/reduce_scatter | solution.py:238
  285.6 19.4 %copy-start.2 = (f32[512,3072]{1,0:T(8,128)S(1)}, f32[512,3072]{1,0:T(8,128)}, u32[]{:S(2)}) copy-start(f32[512,3072]{1,0:T(8,128)} %fusion.83) | copy-start | bytes 18874372
  305.0 11.0 %copy-start.8 = (bf16[512,3072]{1,0:T(8,128)(2,1)}, bf16[512,3072]{1,0:T(8,128)(2,1)S(1)}, u32[]{:S(2)}) copy-start(bf16[512,3072]{1,0:T(8,128)(2,1)S(1)} %get-tuple-element.39) | copy-start | bytes 9437188
  332.5 3.0 copy-start.3
  338.5 86.7 %copy-start.18 = (f32[4,128,16]{1,2,0:T(8,128)S(1)}, f32[4,128,16]{1,2,0:T(8,128)}, u32[]{:S(2)}) copy-start(f32[4,128,16]{1,2,0:T(8,128)} %copy-done.17) | copy-start | bytes 98308
  340.6 85.1 %copy-start.16 = (f32[4,128,16]{1,2,0:T(8,128)S(1)}, f32[4,128,16]{1,2,0:T(8,128)}, u32[]{:S(2)}) copy-start(f32[4,128,16]{1,2,0:T(8,128)} %copy-done.15) | copy-start | bytes 98308
  427.0 4.2 copy-start.14
  455.5 310.6 %all-reduce.22.cloned.1.call-start = ((), (), s32[]{:S(2)}) async-start(), calls=%async_computation.10 | async-start | bytes 7077888 | tf_op jit(solution)/shard_map/psum | solution.py:252
  629.0 6.1 copy-start.11
  635.1 5.9 copy-start.1
  635.1 5.9 copy-start.10
  635.1 5.9 copy-start.32
  642.9 5.4 copy-start.28
  642.9 6.5 copy-start.26
  695.3 78.0 %copy-start.33 = (f32[96]{0:T(128)}, f32[96]{0:T(128)S(1)}, u32[]{:S(2)}) copy-start(f32[96]{0:T(128)S(1)} %dynamic_slice.26) | copy-start | bytes 1156
  (12 other events, 16.1 us)
Sparse Core Ops, SparseCore 0:
  9.9 36.8 all-gather.7
  48.7 24.0 all-gather.13
  75.2 46.6 all-gather.11
  124.2 46.6 all-gather.9
  172.7 38.9 all-gather.15
  213.4 38.8 all-gather.17
  265.5 157.4 reduce-scatter.2
  455.7 173.2 reduce-scatter.4
  631.3 134.7 all-reduce.21
where the time goes:
time: 787 us; the launch traced here: 781 us
  waiting for transfers between devices  383 us (49%)
  matrix products  176 us (22%)
  blocking collectives  80.3 us (10%)
  other arithmetic  72.3 us (9%)
  local copies, waits for them, and re-layouts  51.7 us (7%)
  between operations  16.3 us (2%)
    reduce_scatter x1, waiting for transfers between devices, on_device(): lax.psum_scatter(jnp.concatenate([jnp.einsum('rc,rk->ck', input_one, grad...  173 us
    reduce_scatter x1, waiting for transfers between devices, on_device(): lax.psum_scatter(key_terms, 'fsdp', scatter_dimension=1, tiled=True)  82.4 us
    psum x1, waiting for transfers between devices, on_device(): owned = lax.psum(owned, 'rep')  64.2 us
    psum x1, blocking collectives, on_device(): lax.psum((local_vectors[0], local_vectors[1], local_vectors[2], local_vec...  44.4 us
    all_gather x1, waiting for transfers between devices, on_device(): lax.all_gather(key_flat, 'fsdp', axis=1, tiled=True)  37.4 us
    unnamed x1, blocking collectives  26.5 us
    all_gather x1, waiting for transfers between devices, on_device(): lax.all_gather(value_flat, 'fsdp', axis=1, tiled=True)  23.9 us
    dot_general x1, matrix products, on_device(): jnp.einsum('sqhd,skhd->shqk', grad_heads, values, preferred_element_type=...  20.5 us
  transfers between devices with their start and end apart: 9, of which 5 were waited for; matrix products, arithmetic and copies ran while one was open for 33% of the time, Pallas kernels for 0%

commit v1 on v0

--- a/solution.py
+++ b/solution.py
@@ -249,7 +249,7 @@
         scatter_dimension=0,
         tiled=True,
     )
-    owned = lax.psum(owned, "rep")
+    owned = jnp.sum(lax.all_gather(owned, "rep"), axis=0)
     edge_two = qkv_cols + width
     edge_three = edge_two + hidden_cols
     grad_w_qkv = owned[:, :qkv_cols]

time: 787 us -> 899 us (1.14)
  waiting for transfers between devices: 383 us -> 482 us
  blocking collectives: 80.3 us -> 91 us
    all_gather x0 -> x1, waiting for transfers between devices: none -> 162 us  [on_device(): owned = jnp.sum(lax.all_gather(owned, 'rep'), axis=0)]
    psum x1 -> x0, waiting for transfers between devices: 64.2 us -> none  [on_device(): owned = lax.psum(owned, 'rep')]
    psum x1, blocking collectives: 44.4 us -> 55 us  [on_device(): lax.psum((local_vectors[0], local_vectors[1], local_vectors[2], local_vec...]
  transfers between devices with their start and end apart: 9 -> 9, of which waited for: 5 -> 5; matrix products, arithmetic and copies ran while one was open for 33% -> 29% of each run, Pallas kernels for 0% -> 0%
where the time goes in v1:
time: 899 us; the launch traced here: 893 us
  waiting for transfers between devices  482 us (54%)
  matrix products  176 us (20%)
  blocking collectives  91 us (10%)
  other arithmetic  78.7 us (9%)
  local copies, waits for them, and re-layouts  47.6 us (5%)
  between operations  16.4 us (2%)
    reduce_scatter x1, waiting for transfers between devices, on_device(): lax.psum_scatter(jnp.concatenate([jnp.einsum('rc,rk->ck', input_one, grad...  173 us
    all_gather x1, waiting for transfers between devices, on_device(): owned = jnp.sum(lax.all_gather(owned, 'rep'), axis=0)  162 us
    reduce_scatter x1, waiting for transfers between devices, on_device(): lax.psum_scatter(key_terms, 'fsdp', scatter_dimension=1, tiled=True)  82.4 us
    psum x1, blocking collectives, on_device(): lax.psum((local_vectors[0], local_vectors[1], local_vectors[2], local_vec...  55 us
    all_gather x1, waiting for transfers between devices, on_device(): lax.all_gather(key_flat, 'fsdp', axis=1, tiled=True)  37.4 us
    unnamed x1, blocking collectives  26.5 us
    all_gather x1, waiting for transfers between devices, on_device(): lax.all_gather(value_flat, 'fsdp', axis=1, tiled=True)  23.9 us
    dot_general x1, matrix products, on_device(): jnp.einsum('sqhd,skhd->shqk', grad_heads, values, preferred_element_type=...  20.5 us
  transfers between devices with their start and end apart: 9, of which 5 were waited for; matrix products, arithmetic and copies ran while one was open for 29% of the time, Pallas kernels for 0%

profile of v1, /device:TPU:0, one launch (start us, length us, event | category | flops | bytes accessed | tf_op | source)
XLA Modules:
  0.0 892.7 jit_solution(17670693738919725443)
XLA Ops:
  21.0 26.5 %all-reduce.19 = (bf16[768]{0:T(1024)(128)(2,1)S(1)}, bf16[768]{0:T(1024)(128)(2,1)S(1)}, bf16[768]{0:T(1024)(128)(2,1)}, bf16[768]{0:T(1024)(128)(2,1)}, bf16[7...) all-reduce(bf16[768]{0:T(1024)(128)(2,1)S(1)} %dynamic-update-slice, ...), channel_id=1, replica_groups=mesh['rep'=4,'fsdp'=8] {'fsdp'}, use_global_device_ids=true, to_apply=%add.15 | all-reduce | flops 6912 | bytes 27648
  49.2 6.1 convolution_add_fusion
  55.4 6.2 copy.46
  61.5 6.3 reshape.249
  84.6 37.4 %all-gather.14.cloned.1.call-done = bf16[4,1024,768]{1,2,0:T(8,128)(2,1)} async-done(((bf16[4,128,768]{1,2,0:T(8,128)(2,1)}), bf16[4,1024,768]{1,2,0:T(8,128)(2,1)}) %all-gather.14.cloned.1.call-update) | async-done | bytes 6291472 | tf_op jit(solution)/shard_map/all_gather | solution.py:124
  121.9 12.9 %select_reduce_fusion.1 = (f32[4,12,128]{2,1,0:T(8,128)S(1)}, f32[4,12,128,1024]{3,2,1,0:T(8,128)}) fusion(pred[4,128,1024]{2,1,0:T(8,128)(4,1)S(1)} %fusion.13, bf16[4,1024,12,64]{1,3,2,0:T(8,128)(2,1)} %bitcast.165, bf16[4,128,12,48]{1,3,2,0:T(8,128)(2,1)S(1)} %slice.110, bf16[4,128,12,16]{1,3,2,0:T(8,128)(2,1)S(1)} %get-tuple-element.61), kind=kOutput, calls=%fused_computation.6 | convolution fusion | flops 825747456 | bytes 32792576 | tf_op jit(solution)/shard_map/sqhd,skhd->shqk/dot_general | solution.py:107
  134.9 12.2 %select_reduce_fusion = f32[4,12,128]{2,1,0:T(8,128)S(1)} fusion(f32[4,12,128,1024]{3,2,1,0:T(8,128)} %get-tuple-element.76, f32[4,12,128]{2,1,0:T(8,128)S(1)} %broadcast_maximum_fusion, pred[4,128,1024]{2,1,0:T(8,128)(4,1)S(1)} %fusion.13), kind=kLoop, calls=%fused_computation.5 | loop fusion | flops 31451136 | bytes 25739264 | tf_op jit(solution)/shard_map/reduce_sum | solution.py:121
  147.1 23.9 %all-gather.12.cloned.1.call-done = bf16[4,1024,768]{1,2,0:T(8,128)(2,1)} async-done(((bf16[4,128,768]{1,2,0:T(8,128)(2,1)}), bf16[4,1024,768]{1,2,0:T(8,128)(2,1)}) %all-gather.12.cloned.1.call-update) | async-done | bytes 6291472 | tf_op jit(solution)/shard_map/all_gather | solution.py:125
  170.9 14.2 %fusion.58 = f32[4,12,64,128]{3,2,1,0:T(8,128)} fusion(bf16[4,1024,12,64]{1,3,2,0:T(8,128)(2,1)} %bitcast.192, f32[4,12,128,1024]{3,2,1,0:T(8,128)} %get-tuple-element.76, f32[4,12,128]{2,1,0:T(8,128)S(1)} %log_add_fusion, pred[4,128,1024]{2,1,0:T(8,128)(4,1)S(1)} %fusion.13), kind=kOutput, calls=%fused_computation.110 | convolution fusion | flops 830472192 | bytes 33579008 | tf_op jit(solution)/shard_map/shqk,skhd->sqhd/dot_general | solution.py:133
  185.2 15.0 %fusion.16 = f32[4,128,12]{1,2,0:T(8,128)S(1)} fusion(f32[4,12,64,128]{3,2,1,0:T(8,128)} %fusion.58, bf16[4,1024,12,64]{1,3,2,0:T(8,128)(2,1)} %bitcast.193, f32[4,12,128,1024]{3,2,1,0:T(8,128)} %get-tuple-element.76, f32[4,12,128]{2,1,0:T(8,128)S(1)} %log_add_fusion, pred[4,128,1024]{2,1,0:T(8,128)(4,1)S(1)} %fusion.13, bf16[4,128,12,64]{1,0,3,2:T(4,128)(2,1)} %reshape.254), kind=kOutput, calls=%fused_computation.48 | convolution fusion | flops 850913280 | bytes 34390016 | tf_op jit(solution)/shard_map/shqk,skhd->sqhd/dot_general | solution.py:134
  200.2 20.5 %multiply_convert_fusion = bf16[4,12,128,1024]{3,2,1,0:T(8,128)(2,1)} fusion(f32[4,12,128,1024]{3,2,1,0:T(8,128)} %get-tuple-element.76, f32[4,12,128]{2,1,0:T(8,128)S(1)} %bitcast.196, f32[4,12,128]{2,1,0:T(8,128)S(1)} %log_add_fusion, pred[4,128,1024]{2,1,0:T(8,128)(4,1)S(1)} %fusion.13, bf16[4,1024,12,64]{1,3,2,0:T(8,128)(2,1)} %bitcast.194, ...), kind=kOutput, calls=%fused_computation.2 | convolution fusion | flops 843055104 | bytes 45400064 | tf_op jit(solution)/shard_map/sqhd,skhd->shqk/dot_general | solution.py:172
  220.6 11.1 %fusion.50 = f32[4,12,64,1024]{3,2,1,0:T(8,128)} fusion(bf16[4,12,128,1024]{3,2,1,0:T(8,128)(2,1)} %multiply_convert_fusion, bf16[4,128,12,48]{1,3,2,0:T(8,128)(2,1)S(1)} %slice.110, bf16[4,128,12,16]{1,3,2,0:T(8,128)(2,1)S(1)} %get-tuple-element.61), kind=kOutput, calls=%fused_computation.98 | convolution fusion | flops 806879232 | bytes 25952256 | tf_op jit(solution)/shard_map/shqk,sqhd->skhd/dot_general | solution.py:179
  231.8 14.8 %fusion.47 = f32[4,12,64,1024]{3,2,1,0:T(8,128)} fusion(bf16[4,128,12,64]{1,0,3,2:T(4,128)(2,1)S(1)} %copy-done.12, f32[4,12,128,1024]{3,2,1,0:T(8,128)} %get-tuple-element.76, f32[4,12,128]{2,1,0:T(8,128)S(1)} %log_add_fusion, pred[4,128,1024]{2,1,0:T(8,128)(4,1)S(1)} %fusion.13), kind=kOutput, calls=%fused_computation.94 | convolution fusion | flops 830472192 | bytes 39084032 | tf_op jit(solution)/shard_map/shqk,sqhd->skhd/dot_general | solution.py:182
  246.5 18.8 %pad_maximum_fusion.1 = f32[4,1024,1536]{1,2,0:T(8,128)} fusion(f32[4,1024,768]{1,2,0:T(8,128)} %bitcast.164, f32[4,1024,768]{1,2,0:T(8,128)} %bitcast.163), kind=kLoop, calls=%fused_computation.1 | loop fusion | flops 6291456 | bytes 50331648 | tf_op jit(solution)/shard_map/concatenate | solution.py:185
  266.0 9.4 %all-gather.1 = bf16[8,1,384]{2,1,0:T(2,128)(2,1)S(1)} all-gather(bf16[1,1,384]{2,1,0:T(2,128)(2,1)S(1)} %reshape.281), channel_id=1, replica_groups=mesh['rep'=4,'fsdp'=8] {'fsdp'}, dimensions={0}, use_global_device_ids=true | all-gather | bytes 6912 | tf_op jit(solution)/shard_map/all_gather | solution.py:64
  276.7 8.9 fusion.83
  285.6 19.4 %convert_reduce_fusion = (f32[3072]{0:T(1024)S(1)}, bf16[512,3072]{1,0:T(8,128)(2,1)S(1)}, f32[512,3072]{1,0:T(8,128)S(1)}) fusion(f32[512,3072]{1,0:T(8,128)} %fusion.83, f32[3072]{0:T(1024)S(1)} %bitcast.190, bf16[512,768]{1,0:T(8,128)(2,1)S(1)} %bitcast.172, bf16[768,3072]{1,0:T(8,128)(2,1)} %all-gather.20.cloned.1.call-done), kind=kOutput, calls=%fused_computation.12 | convolution fusion | flops 2533880832 | bytes 21258240 | tf_op jit(solution)/shard_map/dot_general | solution.py:155
  305.0 3.2 multiply_convert_fusion.1
  308.2 7.8 convolution_bitcast_fusion
  316.0 5.2 fusion.86
  321.2 11.3 %multiply_bitcast_fusion = f32[4,128,12,64]{1,3,2,0:T(8,128)S(1)} fusion(bf16[4,1024,12,64]{1,3,2,0:T(8,128)(2,1)} %bitcast.166, bf16[4,12,128,1024]{3,2,1,0:T(8,128)(2,1)} %multiply_convert_fusion), kind=kOutput, calls=%fused_computation.82 | convolution fusion | flops 805699584 | bytes 20447232 | tf_op jit(solution)/shard_map/shqk,skhd->sqhd/dot_general | solution.py:176
  340.6 82.4 %reduce-scatter.3.cloned.1.call-done = f32[4,128,1536]{1,2,0:T(8,128)} async-done(((f32[4,1024,1536]{1,2,0:T(8,128)}), f32[4,128,1536]{1,2,0:T(8,128)}) %reduce-scatter.3.cloned.1.call-update) | async-done | bytes 3145744 | tf_op jit(solution)/shard_map/reduce_scatter | solution.py:192
  431.2 4.9 fusion.9
  436.1 19.4 %pad_maximum_fusion = f32[768,9216]{1,0:T(8,128)} fusion(f32[768,3072]{1,0:T(8,128)} %convolution_bitcast_fusion, f32[768,3072]{1,0:T(8,128)} %fusion.86, f32[768,768]{1,0:T(8,128)S(1)} %copy.57, f32[768,2304]{1,0:T(8,128)} %fusion.9), kind=kLoop, calls=%fused_computation | loop fusion | flops 21233664 | bytes 56623104 | tf_op jit(solution)/shard_map/concatenate | solution.py:239
  455.8 173.1 %reduce-scatter.5.cloned.1.call-done = f32[96,9216]{1,0:T(8,128)} async-done(((f32[768,9216]{1,0:T(8,128)}), f32[96,9216]{1,0:T(8,128)}) %reduce-scatter.5.cloned.1.call-update) | async-done | bytes 3538960 | tf_op jit(solution)/shard_map/reduce_scatter | solution.py:238
  629.2 6.1 fusion.85
  635.3 5.7 fusion.84
  642.9 5.7 fusion.76
  651.2 55.0 %all-reduce.18 = (f32[768]{0:T(1024)S(1)}, f32[768]{0:T(1024)S(1)}, f32[768]{0:T(1024)S(1)}, f32[768]{0:T(1024)S(1)}, f32[2304]{0:T(1024)S(1)}, /*index=5*/f32[768]{0:T(1024)S(1)}, f32[3072]{0:T(1024)S(1)}) all-reduce(f32[768]{0:T(1024)S(1)} %get-tuple-element.23, ...), channel_id=1, replica_groups=mesh['rep'=4,'fsdp'=8] {'rep','fsdp'}, use_global_device_ids=true, to_apply=%region_13.14 | all-reduce | flops 9216 | bytes 73728 | tf_op jit(solution)/shard_map/psum | solution.py:220
  710.0 3.0 add_convert_fusion.2
  713.0 162.5 %all-gather.22.cloned.1.call-done = f32[384,9216]{1,0:T(8,128)} async-done(((f32[96,9216]{1,0:T(8,128)}), f32[384,9216]{1,0:T(8,128)}) %all-gather.22.cloned.1.call-update) | async-done | bytes 14155792 | tf_op jit(solution)/shard_map/all_gather | solution.py:252
  875.5 6.4 reduce_sum.156
  (177 shorter events, 61.0 us)
Async XLA Ops:
  7.2 42.0 %all-gather.10.cloned.1.call-start = ((), (), s32[]{:S(2)}) async-start(), calls=%async_computation.2 | async-start | bytes 3981312 | tf_op jit(solution)/shard_map/all_gather | solution.py:76
  7.9 69.8 %all-gather.16.cloned.1.call-start = ((), (), s32[]{:S(2)}) async-start(), calls=%async_computation.5 | async-start | bytes 1327104 | tf_op jit(solution)/shard_map/all_gather | solution.py:138
  8.7 113.3 %all-gather.14.cloned.1.call-start = ((), (), s32[]{:S(2)}) async-start(), calls=%async_computation.4 | async-start | bytes 7077888 | tf_op jit(solution)/shard_map/all_gather | solution.py:124
  10.0 45.3 %copy-start.23 = (f32[512]{0:T(512)}, f32[512]{0:T(512)S(1)}, u32[]{:S(2)}) copy-start(f32[512]{0:T(512)S(1)} %get-tuple-element.73) | copy-start | bytes 6148
  11.6 263.9 %copy-start.27 = (f32[4,128]{1,0:T(4,128)}, f32[4,128]{1,0:T(4,128)S(1)}, u32[]{:S(2)}) copy-start(f32[4,128]{1,0:T(4,128)S(1)} %fusion.28) | copy-start | bytes 6148
  12.5 58.2 %copy-start.15 = (f32[4,128,16]{1,2,0:T(8,128)}, f32[4,128,16]{1,2,0:T(8,128)S(1)}, u32[]{:S(2)}) copy-start(f32[4,128,16]{1,2,0:T(8,128)S(1)} %get-tuple-element.67) | copy-start | bytes 98308
  12.5 58.2 %copy-start.17 = (f32[4,128,16]{1,2,0:T(8,128)}, f32[4,128,16]{1,2,0:T(8,128)S(1)}, u32[]{:S(2)}) copy-start(f32[4,128,16]{1,2,0:T(8,128)S(1)} %get-tuple-element.68) | copy-start | bytes 98308
  47.5 228.0 %copy-start.19 = (f32[768]{0:T(1024)}, f32[768]{0:T(1024)S(1)}, u32[]{:S(2)}) copy-start(f32[768]{0:T(1024)S(1)} %convert_element_type.126) | copy-start | bytes 9220
  47.5 7.9 copy-start.21
  47.6 7.8 copy-start.25
  71.7 6.0 copy-start.5
  72.8 98.1 %all-gather.12.cloned.1.call-start = ((), (), s32[]{:S(2)}) async-start(), calls=%async_computation.3 | async-start | bytes 7077888 | tf_op jit(solution)/shard_map/all_gather | solution.py:125
  75.6 201.1 %all-gather.18.cloned.1.call-start = ((), (), s32[]{:S(2)}) async-start(), calls=%async_computation.6 | async-start | bytes 5308416 | tf_op jit(solution)/shard_map/all_gather | solution.py:77
  76.2 209.3 %all-gather.20.cloned.1.call-start = ((), (), s32[]{:S(2)}) async-start(), calls=%async_computation.7 | async-start | bytes 5308416 | tf_op jit(solution)/shard_map/all_gather | solution.py:139
  76.8 346.2 %reduce-scatter.3.cloned.1.call-start = ((), (), s32[]{:S(2)}) async-start(), calls=%async_computation.8 | async-start | bytes 28311552 | tf_op jit(solution)/shard_map/reduce_scatter | solution.py:192
  220.6 11.1 %copy-start.12 = (bf16[4,128,12,64]{1,0,3,2:T(4,128)(2,1)S(1)}, bf16[4,128,12,64]{1,0,3,2:T(4,128)(2,1)}, u32[]{:S(2)}) copy-start(bf16[4,128,12,64]{1,0,3,2:T(4,128)(2,1)} %reshape.254) | copy-start | bytes 2359300
  265.3 10.1 %copy-start = (bf16[4,128,768]{2,1,0:T(8,128)(2,1)S(1)}, bf16[4,128,768]{2,1,0:T(8,128)(2,1)}, u32[]{:S(2)}) copy-start(bf16[4,128,768]{2,1,0:T(8,128)(2,1)} %param.15) | copy-start | bytes 2359300
  265.3 363.6 %reduce-scatter.5.cloned.1.call-start = ((), (), s32[]{:S(2)}) async-start(), calls=%async_computation.9 | async-start | bytes 31850496 | tf_op jit(solution)/shard_map/reduce_scatter | solution.py:238
  285.6 19.4 %copy-start.2 = (f32[512,3072]{1,0:T(8,128)S(1)}, f32[512,3072]{1,0:T(8,128)}, u32[]{:S(2)}) copy-start(f32[512,3072]{1,0:T(8,128)} %fusion.83) | copy-start | bytes 18874372
  305.0 11.0 %copy-start.8 = (bf16[512,3072]{1,0:T(8,128)(2,1)}, bf16[512,3072]{1,0:T(8,128)(2,1)S(1)}, u32[]{:S(2)}) copy-start(bf16[512,3072]{1,0:T(8,128)(2,1)S(1)} %get-tuple-element.39) | copy-start | bytes 9437188
  338.5 86.7 %copy-start.18 = (f32[4,128,16]{1,2,0:T(8,128)S(1)}, f32[4,128,16]{1,2,0:T(8,128)}, u32[]{:S(2)}) copy-start(f32[4,128,16]{1,2,0:T(8,128)} %copy-done.17) | copy-start | bytes 98308
  340.6 85.1 %copy-start.16 = (f32[4,128,16]{1,2,0:T(8,128)S(1)}, f32[4,128,16]{1,2,0:T(8,128)}, u32[]{:S(2)}) copy-start(f32[4,128,16]{1,2,0:T(8,128)} %copy-done.15) | copy-start | bytes 98308
  455.5 173.5 %copy-start.30 = (bf16[768]{0:T(1024)(128)(2,1)S(1)}, bf16[768]{0:T(1024)(128)(2,1)}, u32[]{:S(2)}) copy-start(bf16[768]{0:T(1024)(128)(2,1)} %get-tuple-element.34) | copy-start | bytes 4612
  455.5 173.5 %copy-start.29 = (bf16[768]{0:T(1024)(128)(2,1)S(1)}, bf16[768]{0:T(1024)(128)(2,1)}, u32[]{:S(2)}) copy-start(bf16[768]{0:T(1024)(128)(2,1)} %get-tuple-element.33) | copy-start | bytes 4612
  455.5 420.0 %all-gather.22.cloned.1.call-start = ((), (), s32[]{:S(2)}) async-start(), calls=%async_computation.10 | async-start | bytes 17694720 | tf_op jit(solution)/shard_map/all_gather | solution.py:252
  629.2 6.1 copy-start.11
  635.2 5.7 copy-start.1
  635.3 5.7 copy-start.10
  635.3 5.7 copy-start.32
  642.9 5.8 copy-start.28
  642.9 6.9 copy-start.26
  706.4 178.8 %copy-start.33 = (f32[96]{0:T(128)}, f32[96]{0:T(128)S(1)}, u32[]{:S(2)}) copy-start(f32[96]{0:T(128)S(1)} %dynamic_slice.26) | copy-start | bytes 1156
  (12 other events, 21.9 us)
Sparse Core Ops, SparseCore 0:
  9.9 36.8 all-gather.9
  48.7 24.0 all-gather.15
  75.2 46.6 all-gather.13
  124.2 46.6 all-gather.11
  172.7 38.9 all-gather.17
  213.4 38.8 all-gather.19
  265.5 157.4 reduce-scatter.2
  455.7 173.2 reduce-scatter.4
  630.5 244.9 all-gather.21
